TPU v7x, 128 devices: a whole 4x4x4 slice. The times are simulated.
128 devices in a mesh: col: 32 (over x, y, core), row: 4 (over z).
Axes of the slice: x: 4, y: 4, z: 4, core: 2. Of those that a mesh axis runs over, the one named last changes fastest.
Arguments:
- rhs: float32 [2, 32, 4, 4096], P(None, None, 'row', 'col'), may hold values from -6 to 6
- u_factor: bfloat16 [64, 160, 2, 256, 128], P('row', 'col'), may hold values from -0.0390625 to 0.0390625
- v_factor: bfloat16 [64, 160, 2, 256, 128], P('row', 'col'), may hold values from -0.375 to 0.375
- ranks: int32 [64, 160], P('row', 'col'), may hold values from 8 to 128, as said below
- assign: int32 [160], replicated, may hold values from 0 to 159, each once
Outputs:
- solution: float32 [2, 32, 40960], P(None, None, 'col')
- residual_estimate: float32 [32], replicated
Inputs may be any that keep to these rules, and one draw needn't show every extreme that they name: `ranks`: every entry is 128 // 16 times a power of two from 1 to 16.
All inputs are finite; a program needn't handle non-finite values.
Results may differ from a plain program's by a relative error of at most 0.0068.
Values may be sent and summed in bfloat16 or wider, within the bound.
A program may use at most 128 MiB of HBM per device.

v0:
```python
import jax
import jax.numpy as jnp
from jax import lax
from jax.sharding import Mesh
from jax.sharding import PartitionSpec as P

ITERS = 2
COL = ("col_0", "col_1", "col_2")
COL_ROW = ("col_0", "col_1", "col_2", "row")


def cut_along(x, dim, devices):
    before, after = (x.shape[:dim], x.shape[dim + 1 :])
    return jnp.moveaxis(x.reshape(*before, devices, -1, *after), dim, 0)


def sent_and_summed(x, axis, dim):
    devices = lax.axis_size(axis)
    tiles = lax.all_to_all(cut_along(x, dim, devices), axis, 0, 0, tiled=True)
    return jnp.sum(tiles.astype(jnp.float32), axis=0)


def in_order(tiles, dim):
    tiles = jnp.moveaxis(tiles, 0, dim)
    dims = tiles.shape
    return tiles.reshape(*dims[:dim], dims[dim] * dims[dim + 1], *dims[dim + 2 :])


def copy_for_each(x, axis):
    copies = jnp.broadcast_to(x, (lax.axis_size(axis), *x.shape))
    return lax.all_to_all(copies, axis, split_axis=0, concat_axis=0, tiled=True)


def collect(x, axis, dim):
    return in_order(copy_for_each(x, axis), dim)


def by_axis(x, axes):
    for axis in axes:
        x = lax.psum(x, axis)
    return x


def over_copies(x, axis):
    everything = copy_for_each(x, axis)
    return jnp.sum(everything.astype(jnp.float32), axis=0)


def over_copies_2(x, axis):
    everything = copy_for_each(x, axis)
    return jnp.sum(everything, axis=0)


def sum_squares(value):
    return jnp.sum(value * value, axis=(0, 2))


def on_device(rhs, u_factor, v_factor, ranks, assign):
    tile_rows = u_factor.shape[0]
    tile_cols = u_factor.shape[1]
    tile_size = u_factor.shape[3]
    rank_cap = u_factor.shape[4]
    sources = rhs.shape[1]
    rank_iota = lax.broadcasted_iota(jnp.int32, (tile_rows, tile_cols, 1, 1, rank_cap), 4)
    mask = (rank_iota < ranks[:, :, None, None, None]).astype(jnp.float32)

    def adjoint_terms(group_data):
        data_b = group_data.reshape(2, sources, tile_rows, tile_size)
        raw = jnp.einsum("ipcnk,dsin->ipcdsk", u_factor, data_b, preferred_element_type=jnp.float32)
        coeff = jnp.stack(
            [raw[:, :, 0, 0] + raw[:, :, 1, 1], raw[:, :, 0, 1] - raw[:, :, 1, 0]], axis=2
        )
        coeff = (coeff * mask).astype(jnp.bfloat16)
        prod = jnp.einsum("ipcnk,ipdsk->cdspn", v_factor, coeff, preferred_element_type=jnp.float32)
        partial_model = jnp.stack([prod[0, 0] + prod[1, 1], prod[0, 1] - prod[1, 0]], axis=0)
        return partial_model.reshape(2, sources, tile_cols * tile_size)

    def adjoint_step(data_hat, v_prev):
        group_data = collect(data_hat.astype(jnp.bfloat16), COL, 2)
        beta_now = jnp.sqrt(by_axis(sum_squares(data_hat), COL_ROW))
        model_sum = over_copies(adjoint_terms(group_data).astype(jnp.bfloat16), "row").astype(
            jnp.float32
        )
        v_hat = model_sum / beta_now[None, :, None] - beta_now[None, :, None] * v_prev
        alpha_now = jnp.sqrt(over_copies_2(sum_squares(v_hat), COL))
        return (
            data_hat / beta_now[None, :, None],
            beta_now,
            v_hat / alpha_now[None, :, None],
            alpha_now,
        )

    data_first = rhs.reshape(2, sources, rhs.shape[3])
    zero_model = jnp.zeros((2, sources, tile_cols * tile_size), jnp.float32)
    u_vec, beta_now, v_vec, alpha_now = adjoint_step(data_first, zero_model)
    w_vec = v_vec
    x_vec = zero_model
    phibar = beta_now
    rhobar = alpha_now
    for iteration in range(ITERS):
        model_b = v_vec.astype(jnp.bfloat16).reshape(2, sources, tile_cols, tile_size)
        forward_raw = jnp.einsum(
            "ipcnk,dspn->ipcdsk", v_factor, model_b, preferred_element_type=jnp.float32
        )
        forward_coeff = jnp.stack(
            [
                forward_raw[:, :, 0, 0] - forward_raw[:, :, 1, 1],
                forward_raw[:, :, 0, 1] + forward_raw[:, :, 1, 0],
            ],
            axis=2,
        )
        forward_coeff = (forward_coeff * mask).astype(jnp.bfloat16)
        forward_prod = jnp.einsum(
            "ipcnk,ipdsk->cdsin", u_factor, forward_coeff, preferred_element_type=jnp.float32
        )
        partial_data = jnp.stack(
            [forward_prod[0, 0] - forward_prod[1, 1], forward_prod[0, 1] + forward_prod[1, 0]],
            axis=0,
        )
        partial_data = partial_data.reshape(2, sources, tile_rows * tile_size)
        data_hat = (
            sent_and_summed(partial_data.astype(jnp.bfloat16), COL, 2)
            - alpha_now[None, :, None] * u_vec
        )
        u_vec, beta_now, v_vec, alpha_now = adjoint_step(data_hat, v_vec)
        rho_now = jnp.sqrt(rhobar * rhobar + beta_now * beta_now)
        cosine = rhobar / rho_now
        sine = beta_now / rho_now
        theta = sine * alpha_now
        rhobar = -cosine * alpha_now
        phi_now = cosine * phibar
        phibar = sine * phibar
        x_vec = x_vec + (phi_now / rho_now)[None, :, None] * w_vec
        w_vec = v_vec - (theta / rho_now)[None, :, None] * w_vec
    all_cols = assign.shape[0]
    natural = lax.axis_index(COL) * tile_cols + jnp.arange(tile_cols, dtype=jnp.int32)
    positions = jnp.arange(all_cols, dtype=jnp.int32)
    where_held = jnp.sum(
        positions[None, :] * (assign[None, :] == natural[:, None]).astype(jnp.int32), axis=1
    )
    share = sources // lax.axis_size("row")
    own_share = lax.dynamic_slice_in_dim(x_vec, lax.axis_index("row") * share, share, 1)
    gathered = collect(own_share, COL, 2)
    gathered = gathered.reshape(2, share, all_cols, tile_size)
    picked = jnp.take(gathered, where_held, axis=2).reshape(2, share, tile_cols * tile_size)
    solution = collect(picked, "row", 1)
    return (solution, phibar)


def solution(mesh):
    split = Mesh(
        mesh.devices.reshape(4, 4, 2, mesh.shape["row"]), ("col_0", "col_1", "col_2", "row")
    )
    placed = (
        P(None, None, "row", COL),
        P("row", COL, None, None, None),
        P("row", COL, None, None, None),
        P("row", COL),
        P(),
    )
    return jax.shard_map(
        on_device, mesh=split, in_specs=placed, out_specs=(P(None, None, COL), P()), check_vma=False
    )
```

profile of v0, /device:TPU:0, one launch (start us, length us, event | category | flops | bytes accessed | tf_op | source)
XLA Modules:
  0.0 301.4 jit_solution(13848021169827376200)
XLA Ops:
  0.6 0.8 convert_element_type.53
  1.4 0.9 broadcast_in_dim.61
  2.3 7.4 %all-to-all-start = ((bf16[32,2,32,128]{3,2,1,0:T(8,128)(2,1)}), bf16[32,2,32,128]{3,2,1,0:T(8,128)(2,1)S(1)}, u32[]{:S(2)}, u32[]{:S(2)}) async-start(bf16[32,2,32,128]{3,2,1,0:T(8,128)(2,1)} %broadcast_in_dim.61), calls=%async_computation | async-start | bytes 1048576 | tf_op jit(solution)/shard_map/all_to_all | solution.py:31
  9.7 0.8 copy.231
  10.6 10.3 %all-to-all-done = bf16[32,2,32,128]{3,2,1,0:T(8,128)(2,1)S(1)} async-done(((bf16[32,2,32,128]{3,2,1,0:T(8,128)(2,1)}), bf16[32,2,32,128]{3,2,1,0:T(8,128)(2,1)S(1)}, u32[]{:S(2)}, u32[]{:S(2)}) %all-to-all-start) | async-done | bytes 524320 | tf_op jit(solution)/shard_map/all_to_all | solution.py:31
  20.9 0.3 copy.227
  21.3 0.2 reshape_reshape.9
  21.5 6.0 %fusion.29 = f32[16,5,2,2,32,128]{5,4,2,1,3,0:T(8,128)S(1)} fusion(bf16[16,5,2,256,128]{4,3,2,1,0:T(8,128)(2,1)} %param.6, bf16[2,32,16,256,1,1]{3,2,1,0,5,4:T(8,128)(2,1)S(1)} %bitcast.189), kind=kOutput, calls=%fused_computation.28 | convolution fusion | flops 671088640 | bytes 16252928 | tf_op jit(solution)/shard_map/ipcnk,dsin->ipcdsk/dot_general | solution.py:69
  27.4 0.3 fusion.48
  27.7 0.3 fusion.50
  28.0 0.3 slice-done.8
  28.3 3.3 %fusion.55 = f32[2,2,32,5,256]{4,2,0,1,3:T(8,128)S(1)} fusion(bf16[16,5,2,256,128]{4,3,2,1,0:T(8,128)(2,1)S(1)} %bitcast.181, f32[16,5,1,32,128]{4,3,1,0,2:T(8,128)S(1)} %fusion.48, f32[16,5,1,32,128]{4,3,1,0,2:T(8,128)S(1)} %fusion.50, f32[16,5,128]{2,1,0:T(8,128)S(1)} %fusion.88), kind=kOutput, calls=%fused_computation.59 | convolution fusion | flops 673054720 | bytes 13803520 | tf_op jit(solution)/shard_map/ipcnk,ipdsk->cdspn/dot_general | solution.py:74
  32.0 0.9 broadcast_in_dim.62
  32.9 5.3 %all-to-all-start.1 = ((bf16[4,2,32,1280]{3,2,1,0:T(8,128)(2,1)}), bf16[4,2,32,1280]{3,2,1,0:T(8,128)(2,1)S(1)}, u32[]{:S(2)}, u32[]{:S(2)}) async-start(bf16[4,2,32,1280]{3,2,1,0:T(8,128)(2,1)} %broadcast_in_dim.62), calls=%async_computation.1 | async-start | bytes 1310720 | tf_op jit(solution)/shard_map/all_to_all | solution.py:31
  38.3 8.9 %psum.84 = f32[32]{0:T(128)S(1)} all-reduce(f32[32]{0:T(128)S(1)} %multiply_reduce_fusion.4), channel_id=1, replica_groups=mesh['col_0'=4,'col_1'=4,'col_2'=2,'row'=4] {'col_0'}, use_global_device_ids=true, to_apply=%region_3.0 | all-reduce | flops 32 | bytes 256 | tf_op jit(solution)/shard_map/psum | solution.py:40
  47.2 9.2 %psum.85 = f32[32]{0:T(128)S(1)} all-reduce(f32[32]{0:T(128)S(1)} %psum.84), channel_id=1, replica_groups=mesh['col_0'=4,'col_1'=4,'col_2'=2,'row'=4] {'col_1'}, use_global_device_ids=true, to_apply=%region_4.0 | all-reduce | flops 32 | bytes 256 | tf_op jit(solution)/shard_map/psum | solution.py:40
  56.4 2.4 psum.86
  58.9 10.9 %psum.87 = f32[32]{0:T(128)S(1)} all-reduce(f32[32]{0:T(128)S(1)} %psum.86), channel_id=1, replica_groups=mesh['col_0'=4,'col_1'=4,'col_2'=2,'row'=4] {'row'}, use_global_device_ids=true, to_apply=%region_6.0 | all-reduce | flops 32 | bytes 256 | tf_op jit(solution)/shard_map/psum | solution.py:40
  69.9 0.2 multiply_reduce_fusion.1
  70.2 10.5 %all_to_all.52 = f32[32,1,32]{2,1,0:T(1,128)S(1)} all-to-all(f32[32,1,32]{2,1,0:T(1,128)S(1)} %broadcast_in_dim.64), channel_id=1, replica_groups=mesh['col_0'=4,'col_1'=4,'col_2'=2,'row'=4] {'col_0','col_1','col_2'}, dimensions={0} | all-to-all | bytes 8192 | tf_op jit(solution)/shard_map/all_to_all | solution.py:31
  80.7 5.3 %fusion.20 = f32[16,5,2,2,32,128]{5,4,1,0,3,2:T(8,128)S(1)} fusion(f32[2,4,5,8,256]{4,3,2,1,0:T(8,128)S(1)} %bitcast.185, f32[32]{0:T(128)S(1)} %sqrt.30, f32[32]{0:T(128)S(1)} %get-tuple-element.29, f32[32]{0:T(128)S(1)} %get-tuple-element.28, bf16[16,5,2,256,128]{4,3,2,1,0:T(8,128)(2,1)} %param.7), kind=kOutput, calls=%fused_computation.25 | convolution fusion | flops 671416320 | bytes 16056704 | tf_op jit(solution)/shard_map/ipcnk,dspn->ipcdsk/dot_general | solution.py:102
  86.0 1.7 fusion.47
  87.7 4.6 %fusion.32 = f32[2,2,32,16,256]{4,2,0,1,3:T(8,128)S(1)} fusion(bf16[16,5,2,256,128]{4,3,2,1,0:T(8,128)(2,1)S(1)} %bitcast.177, f32[16,5,1,32,128]{4,3,1,0,2:T(8,128)} %get-tuple-element.16, f32[16,5,1,32,128]{4,3,1,0,2:T(8,128)S(1)} %get-tuple-element.15, f32[16,5,128]{2,1,0:T(8,128)S(1)} %fusion.88), kind=kOutput, calls=%fused_computation.29 | convolution fusion | flops 673054720 | bytes 15245312 | tf_op jit(solution)/shard_map/ipcnk,ipdsk->cdsin/dot_general | solution.py:113
  93.1 0.2 copy.245
  93.3 14.5 %all_to_all.53 = bf16[32,2,32,128]{3,2,1,0:T(8,128)(2,1)S(1)} all-to-all(bf16[32,2,32,128]{3,2,1,0:T(8,128)(2,1)S(1)} %copy.245), channel_id=1, replica_groups=mesh['col_0'=4,'col_1'=4,'col_2'=2,'row'=4] {'col_0','col_1','col_2'}, dimensions={0} | all-to-all | bytes 1048576 | tf_op jit(solution)/shard_map/all_to_all | solution.py:19
  107.9 0.2 multiply_reduce_fusion.3
  108.2 15.0 %all_to_all.54 = bf16[32,2,32,128]{3,2,1,0:T(8,128)(2,1)S(1)} all-to-all(bf16[32,2,32,128]{3,2,1,0:T(8,128)(2,1)S(1)} %broadcast_in_dim.65), channel_id=1, replica_groups=mesh['col_0'=4,'col_1'=4,'col_2'=2,'row'=4] {'col_0','col_1','col_2'}, dimensions={0} | all-to-all | bytes 1048576 | tf_op jit(solution)/shard_map/all_to_all | solution.py:31
  123.2 0.3 copy.246
  123.8 5.3 %fusion.26 = f32[16,5,2,2,32,128]{5,4,1,0,3,2:T(8,128)S(1)} fusion(bf16[2,32,16,256,1,1]{3,2,1,0,5,4:T(8,128)(2,1)S(1)} %bitcast.187, bf16[16,5,2,256,128]{4,3,2,1,0:T(8,128)(2,1)} %param.6), kind=kOutput, calls=%fused_computation.27 | convolution fusion | flops 671088640 | bytes 16252928 | tf_op jit(solution)/shard_map/ipcnk,dsin->ipcdsk/dot_general | solution.py:69
  129.1 0.6 fusion.45
  129.8 0.7 slice-done.11
  130.5 3.3 %fusion.60 = f32[2,2,32,5,256]{4,2,0,1,3:T(8,128)S(1)} fusion(bf16[16,5,2,256,128]{4,3,2,1,0:T(8,128)(2,1)S(1)} %bitcast.183, f32[16,5,1,32,128]{4,3,1,0,2:T(8,128)S(1)} %get-tuple-element.14, f32[16,5,1,32,128]{4,3,1,0,2:T(8,128)S(1)} %get-tuple-element.13, f32[16,5,128]{2,1,0:T(8,128)S(1)} %copy-done.2), kind=kOutput, calls=%fused_computation.60 | convolution fusion | flops 673054720 | bytes 13803520 | tf_op jit(solution)/shard_map/ipcnk,ipdsk->cdspn/dot_general | solution.py:74
  134.1 0.9 broadcast_in_dim.66
  135.0 3.5 %all-to-all-start.5 = ((bf16[4,2,32,1280]{3,2,1,0:T(8,128)(2,1)}), bf16[4,2,32,1280]{3,2,1,0:T(8,128)(2,1)S(1)}, u32[]{:S(2)}, u32[]{:S(2)}) async-start(bf16[4,2,32,1280]{3,2,1,0:T(8,128)(2,1)} %broadcast_in_dim.66), calls=%async_computation.5 | async-start | bytes 1310720 | tf_op jit(solution)/shard_map/all_to_all | solution.py:31
  138.5 8.9 %psum.88 = f32[32]{0:T(128)S(1)} all-reduce(f32[32]{0:T(128)S(1)} %get-tuple-element.9), channel_id=1, replica_groups=mesh['col_0'=4,'col_1'=4,'col_2'=2,'row'=4] {'col_0'}, use_global_device_ids=true, to_apply=%region_11.0 | all-reduce | flops 32 | bytes 256 | tf_op jit(solution)/shard_map/psum | solution.py:40
  147.4 9.2 %psum.89 = f32[32]{0:T(128)S(1)} all-reduce(f32[32]{0:T(128)S(1)} %psum.88), channel_id=1, replica_groups=mesh['col_0'=4,'col_1'=4,'col_2'=2,'row'=4] {'col_1'}, use_global_device_ids=true, to_apply=%region_12.0 | all-reduce | flops 32 | bytes 256 | tf_op jit(solution)/shard_map/psum | solution.py:40
  156.6 2.4 psum.90
  159.1 10.9 %psum.91 = f32[32]{0:T(128)S(1)} all-reduce(f32[32]{0:T(128)S(1)} %psum.90), channel_id=1, replica_groups=mesh['col_0'=4,'col_1'=4,'col_2'=2,'row'=4] {'row'}, use_global_device_ids=true, to_apply=%region_14.0 | all-reduce | flops 32 | bytes 256 | tf_op jit(solution)/shard_map/psum | solution.py:40
  170.1 1.1 multiply_reduce_fusion
  171.2 10.3 %all_to_all.55 = f32[32,1,32]{2,1,0:T(1,128)S(1)} all-to-all(f32[32,1,32]{2,1,0:T(1,128)S(1)} %broadcast_in_dim.67), channel_id=1, replica_groups=mesh['col_0'=4,'col_1'=4,'col_2'=2,'row'=4] {'col_0','col_1','col_2'}, dimensions={0} | all-to-all | bytes 8192 | tf_op jit(solution)/shard_map/all_to_all | solution.py:31
  181.6 5.3 %fusion.23 = f32[16,5,2,2,32,128]{5,4,1,0,3,2:T(8,128)S(1)} fusion(f32[2,4,5,8,256]{4,3,2,1,0:T(8,128)S(1)} %bitcast.188, f32[32]{0:T(128)S(1)} %sqrt.33, f32[32]{0:T(128)S(1)} %sqrt.31, f32[2,4,5,8,256]{4,3,2,1,0:T(8,128)S(1)} %bitcast.186, f32[32]{0:T(128)S(1)} %sqrt.30, f32[32]{0:T(128)S(1)} %get-tuple-element.29, f32[32]{0:T(128)S(1)} %get-tuple-element.28, ...), kind=kOutput, calls=%fused_computation.26 | convolution fusion | flops 671744000 | bytes 16384640 | tf_op jit(solution)/shard_map/ipcnk,dspn->ipcdsk/dot_general | solution.py:102
  186.9 0.6 fusion.43
  187.6 0.5 slice-done.5
  188.1 3.5 %fusion.35 = f32[2,2,32,16,256]{4,2,0,1,3:T(8,128)S(1)} fusion(bf16[16,5,2,256,128]{4,3,2,1,0:T(8,128)(2,1)S(1)} %bitcast.179, f32[16,5,1,32,128]{4,3,1,0,2:T(8,128)S(1)} %get-tuple-element.12, f32[16,5,1,32,128]{4,3,1,0,2:T(8,128)S(1)} %get-tuple-element.11, f32[16,5,128]{2,1,0:T(8,128)S(1)} %copy-done.2), kind=kOutput, calls=%fused_computation.30 | convolution fusion | flops 673054720 | bytes 15245312 | tf_op jit(solution)/shard_map/ipcnk,ipdsk->cdsin/dot_general | solution.py:113
  192.3 1.0 copy.262
  193.3 3.9 %all-to-all-start.7 = ((bf16[32,2,32,128]{3,2,1,0:T(8,128)(2,1)}), bf16[32,2,32,128]{3,2,1,0:T(8,128)(2,1)S(1)}, u32[]{:S(2)}, u32[]{:S(2)}) async-start(bf16[32,2,32,128]{3,2,1,0:T(8,128)(2,1)} %copy.262), calls=%async_computation.7 | async-start | bytes 1048576 | tf_op jit(solution)/shard_map/all_to_all | solution.py:19
  197.3 11.1 %all-to-all-done.7 = bf16[32,2,32,128]{3,2,1,0:T(8,128)(2,1)S(1)} async-done(((bf16[32,2,32,128]{3,2,1,0:T(8,128)(2,1)}), bf16[32,2,32,128]{3,2,1,0:T(8,128)(2,1)S(1)}, u32[]{:S(2)}, u32[]{:S(2)}) %all-to-all-start.7) | async-done | bytes 524320 | tf_op jit(solution)/shard_map/all_to_all | solution.py:19
  208.5 0.2 multiply_reduce_fusion.2
  208.6 8.9 %psum.92 = f32[32]{0:T(128)S(1)} all-reduce(f32[32]{0:T(128)S(1)} %multiply_reduce_fusion.2), channel_id=1, replica_groups=mesh['col_0'=4,'col_1'=4,'col_2'=2,'row'=4] {'col_0'}, use_global_device_ids=true, to_apply=%region_20.0 | all-reduce | flops 32 | bytes 256 | tf_op jit(solution)/shard_map/psum | solution.py:40
  217.6 9.2 %psum.93 = f32[32]{0:T(128)S(1)} all-reduce(f32[32]{0:T(128)S(1)} %psum.92), channel_id=1, replica_groups=mesh['col_0'=4,'col_1'=4,'col_2'=2,'row'=4] {'col_1'}, use_global_device_ids=true, to_apply=%region_21.0 | all-reduce | flops 32 | bytes 256 | tf_op jit(solution)/shard_map/psum | solution.py:40
  226.7 2.4 psum.94
  229.2 7.7 %psum.95 = f32[32]{0:T(128)S(1)} all-reduce(f32[32]{0:T(128)S(1)} %psum.94), channel_id=1, replica_groups=mesh['col_0'=4,'col_1'=4,'col_2'=2,'row'=4] {'row'}, use_global_device_ids=true, to_apply=%region_23.0 | all-reduce | flops 32 | bytes 256 | tf_op jit(solution)/shard_map/psum | solution.py:40
  236.9 0.6 divide_multiply_fusion
  237.7 1.0 fusion.87
  238.7 1.8 broadcast_in_dim.68
  240.5 4.4 %all-to-all-start.8 = ((f32[32,2,8,1280]{3,2,1,0:T(8,128)}), f32[32,2,8,1280]{3,2,1,0:T(8,128)S(1)}, u32[]{:S(2)}, u32[]{:S(2)}) async-start(f32[32,2,8,1280]{3,2,1,0:T(8,128)} %broadcast_in_dim.68), calls=%async_computation.8 | async-start | bytes 5242880 | tf_op jit(solution)/shard_map/all_to_all | solution.py:31
  245.0 0.2 select_reduce_fusion
  245.3 34.1 %all-to-all-done.8 = f32[32,2,8,1280]{3,2,1,0:T(8,128)S(1)} async-done(((f32[32,2,8,1280]{3,2,1,0:T(8,128)}), f32[32,2,8,1280]{3,2,1,0:T(8,128)S(1)}, u32[]{:S(2)}, u32[]{:S(2)}) %all-to-all-start.8) | async-done | bytes 2621472 | tf_op jit(solution)/shard_map/all_to_all | solution.py:31
  279.4 3.0 %copy.263 = f32[2,8,32,1280]{3,2,1,0:T(8,128)} copy(f32[2,8,32,1280]{3,1,0,2:T(8,128)S(1)} %bitcast.184) | data formatting | bytes 5242880 | tf_op jit(solution)/shard_map/transpose | solution.py:24
  282.4 2.7 reshape_reshape.11
  285.1 3.0 %copy.264 = f32[2,8,160,256]{3,1,2,0:T(8,128)} copy(f32[2,8,160,256]{3,2,1,0:T(8,128)S(1)} %reshape_reshape.11) | data formatting | bytes 5242880 | tf_op jit(solution)/shard_map/reshape;reshape | solution.py:144
  288.1 2.3 gather_fusion
  290.5 10.1 %all_to_all.56 = f32[4,2,8,1280]{3,2,1,0:T(8,128)S(1)} all-to-all(f32[4,2,8,1280]{3,2,1,0:T(8,128)S(1)} %broadcast_in_dim.70), channel_id=1, replica_groups=mesh['col_0'=4,'col_1'=4,'col_2'=2,'row'=4] {'row'}, dimensions={0} | all-to-all | bytes 655360 | tf_op jit(solution)/shard_map/all_to_all | solution.py:31
  300.6 0.7 copy.380
  (90 shorter events, 3.7 us)
Async XLA Ops:
  2.3 18.6 %all-to-all-start = ((bf16[32,2,32,128]{3,2,1,0:T(8,128)(2,1)}), bf16[32,2,32,128]{3,2,1,0:T(8,128)(2,1)S(1)}, u32[]{:S(2)}, u32[]{:S(2)}) async-start(bf16[32,2,32,128]{3,2,1,0:T(8,128)(2,1)} %broadcast_in_dim.61), calls=%async_computation | async-start | bytes 1048576 | tf_op jit(solution)/shard_map/all_to_all | solution.py:31
  10.6 77.2 %copy-start.1 = (f32[16,5,128]{2,1,0:T(8,128)}, f32[16,5,128]{2,1,0:T(8,128)S(1)}, u32[]{:S(2)}) copy-start(f32[16,5,128]{2,1,0:T(8,128)S(1)} %fusion.88) | copy-start | bytes 122884
  21.2 6.8 %slice-start.6 = ((s8[10485760]{0:T(1024)(128)(4,1)}), s8[2097152]{0:T(1024)(128)(4,1)S(1)}, s32[]{:S(2)}) async-start(s8[10485760]{0:T(1024)(128)(4,1)} %bitcast.180), calls=%async_computation.16 | async-start | bytes 4194304
  21.4 6.6 %slice-start.7 = ((s8[10485760]{0:T(1024)(128)(4,1)}), s8[4194304]{0:T(1024)(128)(4,1)S(1)}, s32[]{:S(2)}) async-start(s8[10485760]{0:T(1024)(128)(4,1)} %bitcast.180), calls=%async_computation.17 | async-start | bytes 8388608
  21.5 6.9 %slice-start.8 = ((s8[10485760]{0:T(1024)(128)(4,1)}), s8[4194304]{0:T(1024)(128)(4,1)S(1)}, s32[]{:S(2)}) async-start(s8[10485760]{0:T(1024)(128)(4,1)} %bitcast.180), calls=%async_computation.18 | async-start | bytes 8388608
  31.6 6.6 %copy-start = (f32[2,32,1,128]{3,2,1,0:T(1,128)S(1)}, f32[2,32,1,128]{3,2,1,0:T(1,128)}, u32[]{:S(2)}) copy-start(f32[2,32,1,128]{3,2,1,0:T(1,128)} %param.5) | copy-start | bytes 98308
  32.9 36.9 %all-to-all-start.1 = ((bf16[4,2,32,1280]{3,2,1,0:T(8,128)(2,1)}), bf16[4,2,32,1280]{3,2,1,0:T(8,128)(2,1)S(1)}, u32[]{:S(2)}, u32[]{:S(2)}) async-start(bf16[4,2,32,1280]{3,2,1,0:T(8,128)(2,1)} %broadcast_in_dim.62), calls=%async_computation.1 | async-start | bytes 1310720 | tf_op jit(solution)/shard_map/all_to_all | solution.py:31
  69.8 17.9 %slice-start = ((s8[10485760]{0:T(1024)(128)(4,1)}), s8[2097152]{0:T(1024)(128)(4,1)S(1)}, s32[]{:S(2)}) async-start(s8[10485760]{0:T(1024)(128)(4,1)} %bitcast.176), calls=%async_computation.10 | async-start | bytes 4194304
  80.7 7.1 %slice-start.1 = ((s8[10485760]{0:T(1024)(128)(4,1)}), s8[4194304]{0:T(1024)(128)(4,1)S(1)}, s32[]{:S(2)}) async-start(s8[10485760]{0:T(1024)(128)(4,1)} %bitcast.176), calls=%async_computation.11 | async-start | bytes 8388608
  80.7 7.1 %slice-start.2 = ((s8[10485760]{0:T(1024)(128)(4,1)}), s8[4194304]{0:T(1024)(128)(4,1)S(1)}, s32[]{:S(2)}) async-start(s8[10485760]{0:T(1024)(128)(4,1)} %bitcast.176), calls=%async_computation.12 | async-start | bytes 8388608
  123.2 6.5 %slice-start.9 = ((s8[10485760]{0:T(1024)(128)(4,1)}), s8[2097152]{0:T(1024)(128)(4,1)S(1)}, s32[]{:S(2)}) async-start(s8[10485760]{0:T(1024)(128)(4,1)} %bitcast.182), calls=%async_computation.19 | async-start | bytes 4194304
  123.8 6.0 %slice-start.10 = ((s8[10485760]{0:T(1024)(128)(4,1)}), s8[4194304]{0:T(1024)(128)(4,1)S(1)}, s32[]{:S(2)}) async-start(s8[10485760]{0:T(1024)(128)(4,1)} %bitcast.182), calls=%async_computation.20 | async-start | bytes 8388608
  123.8 6.7 %slice-start.11 = ((s8[10485760]{0:T(1024)(128)(4,1)}), s8[4194304]{0:T(1024)(128)(4,1)S(1)}, s32[]{:S(2)}) async-start(s8[10485760]{0:T(1024)(128)(4,1)} %bitcast.182), calls=%async_computation.21 | async-start | bytes 8388608
  129.1 1.4 copy-start.2
  135.0 34.9 %all-to-all-start.5 = ((bf16[4,2,32,1280]{3,2,1,0:T(8,128)(2,1)}), bf16[4,2,32,1280]{3,2,1,0:T(8,128)(2,1)S(1)}, u32[]{:S(2)}, u32[]{:S(2)}) async-start(bf16[4,2,32,1280]{3,2,1,0:T(8,128)(2,1)} %broadcast_in_dim.66), calls=%async_computation.5 | async-start | bytes 1310720 | tf_op jit(solution)/shard_map/all_to_all | solution.py:31
  170.0 17.6 %slice-start.3 = ((s8[10485760]{0:T(1024)(128)(4,1)}), s8[2097152]{0:T(1024)(128)(4,1)S(1)}, s32[]{:S(2)}) async-start(s8[10485760]{0:T(1024)(128)(4,1)} %bitcast.178), calls=%async_computation.13 | async-start | bytes 4194304
  181.5 6.0 %slice-start.4 = ((s8[10485760]{0:T(1024)(128)(4,1)}), s8[4194304]{0:T(1024)(128)(4,1)S(1)}, s32[]{:S(2)}) async-start(s8[10485760]{0:T(1024)(128)(4,1)} %bitcast.178), calls=%async_computation.14 | async-start | bytes 8388608
  181.6 6.5 %slice-start.5 = ((s8[10485760]{0:T(1024)(128)(4,1)}), s8[4194304]{0:T(1024)(128)(4,1)S(1)}, s32[]{:S(2)}) async-start(s8[10485760]{0:T(1024)(128)(4,1)} %bitcast.178), calls=%async_computation.15 | async-start | bytes 8388608
  193.3 15.1 %all-to-all-start.7 = ((bf16[32,2,32,128]{3,2,1,0:T(8,128)(2,1)}), bf16[32,2,32,128]{3,2,1,0:T(8,128)(2,1)S(1)}, u32[]{:S(2)}, u32[]{:S(2)}) async-start(bf16[32,2,32,128]{3,2,1,0:T(8,128)(2,1)} %copy.262), calls=%async_computation.7 | async-start | bytes 1048576 | tf_op jit(solution)/shard_map/all_to_all | solution.py:19
  240.5 4.4 %copy-start.3 = (s32[160]{0:T(256)S(1)}, s32[160]{0:T(256)}, u32[]{:S(2)}) copy-start(s32[160]{0:T(256)} %param.9) | copy-start | bytes 1924
  240.5 38.8 %all-to-all-start.8 = ((f32[32,2,8,1280]{3,2,1,0:T(8,128)}), f32[32,2,8,1280]{3,2,1,0:T(8,128)S(1)}, u32[]{:S(2)}, u32[]{:S(2)}) async-start(f32[32,2,8,1280]{3,2,1,0:T(8,128)} %broadcast_in_dim.68), calls=%async_computation.8 | async-start | bytes 5242880 | tf_op jit(solution)/shard_map/all_to_all | solution.py:31
where the time goes:
time: 303 us; the launch traced here: 301 us
  blocking collectives  152 us (50%)
  waiting for transfers between devices  55.5 us (18%)
  matrix products  36.5 us (12%)
  starting transfers between devices  24.5 us (8%)
  local copies, waits for them, and re-layouts  23 us (8%)
  other arithmetic  8.98 us (3%)
    psum x12, blocking collectives, by_axis(): x = lax.psum(x, axis)  91.2 us
    all_to_all x4, blocking collectives, copy_for_each(): return lax.all_to_all(copies, axis, split_axis=0, concat_axis=0, tiled=True)  46 us
    all_to_all x4, waiting for transfers between devices, copy_for_each(): return lax.all_to_all(copies, axis, split_axis=0, concat_axis=0, tiled=True)  44.4 us
    all_to_all x4, starting transfers between devices, copy_for_each(): return lax.all_to_all(copies, axis, split_axis=0, concat_axis=0, tiled=True)  20.6 us
    all_to_all x1, blocking collectives, sent_and_summed(): tiles = lax.all_to_all(cut_along(x, dim, devices), axis, 0, 0, tiled=True)  14.5 us
    dot_general x2, matrix products, adjoint_terms(): jnp.einsum('ipcnk,dsin->ipcdsk', u_factor, data_b, preferred_element_type...  11.3 us
    all_to_all x1, waiting for transfers between devices, sent_and_summed(): tiles = lax.all_to_all(cut_along(x, dim, devices), axis, 0, 0, tiled=True)  11.1 us
    dot_general x2, matrix products, on_device(): jnp.einsum('ipcnk,dspn->ipcdsk', v_factor, model_b, preferred_element_typ...  10.6 us
  transfers between devices with their start and end apart: 5, of which 3 were waited for; matrix products, arithmetic and copies ran while one was open for 0% of the time, Pallas kernels for 0%

commit v1 on v0

--- a/solution.py
+++ b/solution.py
@@ -37,7 +37,7 @@
 
 def by_axis(x, axes):
     for axis in axes:
-        x = lax.psum(x, axis)
+        x = jnp.sum(lax.all_gather(x, axis), axis=0)
     return x
 
 

time: 303 us -> 312 us (1.030)
  local copies, waits for them, and re-layouts: 23 us -> 29.4 us
    psum x12 -> x0, blocking collectives: 91.2 us -> none  [by_axis(): x = lax.psum(x, axis)]
    unnamed x0 -> x12, blocking collectives: none -> 91 us
    unnamed x33 -> x69, local copies, waits for them, and re-layouts: 2.33 us -> 7.7 us
  transfers between devices with their start and end apart: 5 -> 5, of which waited for: 3 -> 3; matrix products, arithmetic and copies ran while one was open for 0% -> 2% of each run, Pallas kernels for 0% -> 0%
where the time goes in v1:
time: 312 us; the launch traced here: 311 us
  blocking collectives  151 us (48%)
  waiting for transfers between devices  55.7 us (18%)
  matrix products  36.5 us (12%)
  local copies, waits for them, and re-layouts  29.4 us (9%)
  starting transfers between devices  24.3 us (8%)
  other arithmetic  9.24 us (3%)
  between operations  4 us (1%)
    unnamed x12, blocking collectives  91 us
    all_to_all x4, blocking collectives, copy_for_each(): return lax.all_to_all(copies, axis, split_axis=0, concat_axis=0, tiled=True)  46 us
    all_to_all x4, waiting for transfers between devices, copy_for_each(): return lax.all_to_all(copies, axis, split_axis=0, concat_axis=0, tiled=True)  44.6 us
    all_to_all x4, starting transfers between devices, copy_for_each(): return lax.all_to_all(copies, axis, split_axis=0, concat_axis=0, tiled=True)  20.4 us
    all_to_all x1, blocking collectives, sent_and_summed(): tiles = lax.all_to_all(cut_along(x, dim, devices), axis, 0, 0, tiled=True)  14.5 us
    dot_general x2, matrix products, adjoint_terms(): jnp.einsum('ipcnk,dsin->ipcdsk', u_factor, data_b, preferred_element_type...  11.3 us
    all_to_all x1, waiting for transfers between devices, sent_and_summed(): tiles = lax.all_to_all(cut_along(x, dim, devices), axis, 0, 0, tiled=True)  11.1 us
    dot_general x2, matrix products, on_device(): jnp.einsum('ipcnk,dspn->ipcdsk', v_factor, model_b, preferred_element_typ...  10.6 us
  transfers between devices with their start and end apart: 5, of which 3 were waited for; matrix products, arithmetic and copies ran while one was open for 2% of the time, Pallas kernels for 0%

profile of v1, /device:TPU:0, one launch (start us, length us, event | category | flops | bytes accessed | tf_op | source)
XLA Modules:
  0.0 310.5 jit_solution(839607295782500050)
XLA Ops:
  0.6 0.8 convert_element_type.53
  1.4 0.9 broadcast_in_dim.61
  2.3 7.4 %all-to-all-start = ((bf16[32,2,32,128]{3,2,1,0:T(8,128)(2,1)}), bf16[32,2,32,128]{3,2,1,0:T(8,128)(2,1)S(1)}, u32[]{:S(2)}, u32[]{:S(2)}) async-start(bf16[32,2,32,128]{3,2,1,0:T(8,128)(2,1)} %broadcast_in_dim.61), calls=%async_computation | async-start | bytes 1048576 | tf_op jit(solution)/shard_map/all_to_all | solution.py:31
  9.7 0.8 copy.231
  10.6 10.3 %all-to-all-done = bf16[32,2,32,128]{3,2,1,0:T(8,128)(2,1)S(1)} async-done(((bf16[32,2,32,128]{3,2,1,0:T(8,128)(2,1)}), bf16[32,2,32,128]{3,2,1,0:T(8,128)(2,1)S(1)}, u32[]{:S(2)}, u32[]{:S(2)}) %all-to-all-start) | async-done | bytes 524320 | tf_op jit(solution)/shard_map/all_to_all | solution.py:31
  20.9 0.3 copy.227
  21.5 6.0 %fusion.29 = f32[16,5,2,2,32,128]{5,4,2,1,3,0:T(8,128)S(1)} fusion(bf16[16,5,2,256,128]{4,3,2,1,0:T(8,128)(2,1)} %param.6, bf16[2,32,16,256,1,1]{3,2,1,0,5,4:T(8,128)(2,1)S(1)} %bitcast.193), kind=kOutput, calls=%fused_computation.28 | convolution fusion | flops 671088640 | bytes 16252928 | tf_op jit(solution)/shard_map/ipcnk,dsin->ipcdsk/dot_general | solution.py:69
  27.4 0.3 fusion.48
  27.7 0.3 fusion.50
  28.0 0.3 slice-done.8
  28.3 3.3 %fusion.55 = f32[2,2,32,5,256]{4,2,0,1,3:T(8,128)S(1)} fusion(bf16[16,5,2,256,128]{4,3,2,1,0:T(8,128)(2,1)S(1)} %bitcast.185, f32[16,5,1,32,128]{4,3,1,0,2:T(8,128)S(1)} %fusion.48, f32[16,5,1,32,128]{4,3,1,0,2:T(8,128)S(1)} %fusion.50, f32[16,5,128]{2,1,0:T(8,128)S(1)} %fusion.88), kind=kOutput, calls=%fused_computation.59 | convolution fusion | flops 673054720 | bytes 13803520 | tf_op jit(solution)/shard_map/ipcnk,ipdsk->cdspn/dot_general | solution.py:74
  32.1 0.9 broadcast_in_dim.62
  32.9 5.3 %all-to-all-start.1 = ((bf16[4,2,32,1280]{3,2,1,0:T(8,128)(2,1)}), bf16[4,2,32,1280]{3,2,1,0:T(8,128)(2,1)S(1)}, u32[]{:S(2)}, u32[]{:S(2)}) async-start(bf16[4,2,32,1280]{3,2,1,0:T(8,128)(2,1)} %broadcast_in_dim.62), calls=%async_computation.1 | async-start | bytes 1310720 | tf_op jit(solution)/shard_map/all_to_all | solution.py:31
  38.3 0.6 dynamic-slice
  39.6 0.2 dynamic-update-slice
  39.9 8.8 %all-reduce = f32[128]{0:T(128)S(1)} all-reduce(f32[128]{0:T(128)S(1)} %dynamic-update-slice), channel_id=2, replica_groups=mesh['col_0'=4,'col_1'=4,'col_2'=2,'row'=4] {'col_0'}, use_global_device_ids=true, to_apply=%add | all-reduce | flops 128 | bytes 1024
  48.8 0.6 dynamic-slice.1
  50.1 0.2 dynamic-update-slice.1
  50.3 9.2 %all-reduce.1 = f32[128]{0:T(128)S(1)} all-reduce(f32[128]{0:T(128)S(1)} %dynamic-update-slice.1), channel_id=3, replica_groups=mesh['col_0'=4,'col_1'=4,'col_2'=2,'row'=4] {'col_1'}, use_global_device_ids=true, to_apply=%add.1 | all-reduce | flops 128 | bytes 1024
  59.6 0.6 dynamic-slice.2
  61.1 2.4 all-reduce.2
  63.7 0.6 dynamic-slice.3
  65.3 10.9 %all-reduce.3 = f32[128]{0:T(128)S(1)} all-reduce(f32[128]{0:T(128)S(1)} %dynamic-update-slice.3), channel_id=5, replica_groups=mesh['col_0'=4,'col_1'=4,'col_2'=2,'row'=4] {'row'}, use_global_device_ids=true, to_apply=%add.3 | all-reduce | flops 128 | bytes 1024
  76.7 10.5 %all_to_all.55 = f32[32,1,32]{2,1,0:T(1,128)S(1)} all-to-all(f32[32,1,32]{2,1,0:T(1,128)S(1)} %broadcast_in_dim.64), channel_id=1, replica_groups=mesh['col_0'=4,'col_1'=4,'col_2'=2,'row'=4] {'col_0','col_1','col_2'}, dimensions={0} | all-to-all | bytes 8192 | tf_op jit(solution)/shard_map/all_to_all | solution.py:31
  87.2 5.3 %fusion.20 = f32[16,5,2,2,32,128]{5,4,1,0,3,2:T(8,128)S(1)} fusion(f32[2,4,5,8,256]{4,3,2,1,0:T(8,128)S(1)} %bitcast.189, f32[32]{0:T(128)S(1)} %sqrt.88, f32[32]{0:T(128)S(1)} %get-tuple-element.29, f32[32]{0:T(128)S(1)} %get-tuple-element.28, bf16[16,5,2,256,128]{4,3,2,1,0:T(8,128)(2,1)} %param.7), kind=kOutput, calls=%fused_computation.25 | convolution fusion | flops 671416320 | bytes 16056704 | tf_op jit(solution)/shard_map/ipcnk,dspn->ipcdsk/dot_general | solution.py:102
  92.5 1.7 fusion.47
  94.2 4.6 %fusion.32 = f32[2,2,32,16,256]{4,2,0,1,3:T(8,128)S(1)} fusion(bf16[16,5,2,256,128]{4,3,2,1,0:T(8,128)(2,1)S(1)} %bitcast.181, f32[16,5,1,32,128]{4,3,1,0,2:T(8,128)} %get-tuple-element.16, f32[16,5,1,32,128]{4,3,1,0,2:T(8,128)S(1)} %get-tuple-element.15, f32[16,5,128]{2,1,0:T(8,128)S(1)} %fusion.88), kind=kOutput, calls=%fused_computation.29 | convolution fusion | flops 673054720 | bytes 15245312 | tf_op jit(solution)/shard_map/ipcnk,ipdsk->cdsin/dot_general | solution.py:113
  99.8 14.5 %all_to_all.52 = bf16[32,2,32,128]{3,2,1,0:T(8,128)(2,1)S(1)} all-to-all(bf16[32,2,32,128]{3,2,1,0:T(8,128)(2,1)S(1)} %copy.245), channel_id=1, replica_groups=mesh['col_0'=4,'col_1'=4,'col_2'=2,'row'=4] {'col_0','col_1','col_2'}, dimensions={0} | all-to-all | bytes 1048576 | tf_op jit(solution)/shard_map/all_to_all | solution.py:19
  114.7 15.0 %all_to_all.53 = bf16[32,2,32,128]{3,2,1,0:T(8,128)(2,1)S(1)} all-to-all(bf16[32,2,32,128]{3,2,1,0:T(8,128)(2,1)S(1)} %broadcast_in_dim.65), channel_id=1, replica_groups=mesh['col_0'=4,'col_1'=4,'col_2'=2,'row'=4] {'col_0','col_1','col_2'}, dimensions={0} | all-to-all | bytes 1048576 | tf_op jit(solution)/shard_map/all_to_all | solution.py:31
  129.7 0.3 copy.246
  130.3 5.3 %fusion.26 = f32[16,5,2,2,32,128]{5,4,1,0,3,2:T(8,128)S(1)} fusion(bf16[2,32,16,256,1,1]{3,2,1,0,5,4:T(8,128)(2,1)S(1)} %bitcast.191, bf16[16,5,2,256,128]{4,3,2,1,0:T(8,128)(2,1)} %param.6), kind=kOutput, calls=%fused_computation.27 | convolution fusion | flops 671088640 | bytes 16252928 | tf_op jit(solution)/shard_map/ipcnk,dsin->ipcdsk/dot_general | solution.py:69
  135.6 0.6 fusion.45
  136.3 0.7 slice-done.11
  136.9 3.3 %fusion.60 = f32[2,2,32,5,256]{4,2,0,1,3:T(8,128)S(1)} fusion(bf16[16,5,2,256,128]{4,3,2,1,0:T(8,128)(2,1)S(1)} %bitcast.187, f32[16,5,1,32,128]{4,3,1,0,2:T(8,128)S(1)} %get-tuple-element.14, f32[16,5,1,32,128]{4,3,1,0,2:T(8,128)S(1)} %get-tuple-element.13, f32[16,5,128]{2,1,0:T(8,128)S(1)} %copy-done.2), kind=kOutput, calls=%fused_computation.60 | convolution fusion | flops 673054720 | bytes 13803520 | tf_op jit(solution)/shard_map/ipcnk,ipdsk->cdspn/dot_general | solution.py:74
  140.6 0.9 broadcast_in_dim.66
  141.5 3.5 %all-to-all-start.5 = ((bf16[4,2,32,1280]{3,2,1,0:T(8,128)(2,1)}), bf16[4,2,32,1280]{3,2,1,0:T(8,128)(2,1)S(1)}, u32[]{:S(2)}, u32[]{:S(2)}) async-start(bf16[4,2,32,1280]{3,2,1,0:T(8,128)(2,1)} %broadcast_in_dim.66), calls=%async_computation.5 | async-start | bytes 1310720 | tf_op jit(solution)/shard_map/all_to_all | solution.py:31
  145.2 8.8 %all-reduce.4 = f32[128]{0:T(128)S(1)} all-reduce(f32[128]{0:T(128)S(1)} %dynamic-update-slice.4), channel_id=6, replica_groups=mesh['col_0'=4,'col_1'=4,'col_2'=2,'row'=4] {'col_0'}, use_global_device_ids=true, to_apply=%add.4 | all-reduce | flops 128 | bytes 1024
  154.4 9.2 %all-reduce.5 = f32[128]{0:T(128)S(1)} all-reduce(f32[128]{0:T(128)S(1)} %dynamic-update-slice.5), channel_id=7, replica_groups=mesh['col_0'=4,'col_1'=4,'col_2'=2,'row'=4] {'col_1'}, use_global_device_ids=true, to_apply=%add.5 | all-reduce | flops 128 | bytes 1024
  164.0 2.4 all-reduce.6
  166.8 10.8 %all-reduce.7 = f32[128]{0:T(128)S(1)} all-reduce(f32[128]{0:T(128)S(1)} %dynamic-update-slice.7), channel_id=9, replica_groups=mesh['col_0'=4,'col_1'=4,'col_2'=2,'row'=4] {'row'}, use_global_device_ids=true, to_apply=%add.7 | all-reduce | flops 128 | bytes 1024
  177.9 1.1 multiply_reduce_fusion
  179.0 10.3 %all_to_all.56 = f32[32,1,32]{2,1,0:T(1,128)S(1)} all-to-all(f32[32,1,32]{2,1,0:T(1,128)S(1)} %broadcast_in_dim.67), channel_id=1, replica_groups=mesh['col_0'=4,'col_1'=4,'col_2'=2,'row'=4] {'col_0','col_1','col_2'}, dimensions={0} | all-to-all | bytes 8192 | tf_op jit(solution)/shard_map/all_to_all | solution.py:31
  189.4 5.3 %fusion.23 = f32[16,5,2,2,32,128]{5,4,1,0,3,2:T(8,128)S(1)} fusion(f32[2,4,5,8,256]{4,3,2,1,0:T(8,128)S(1)} %bitcast.192, f32[32]{0:T(128)S(1)} %sqrt.91, f32[32]{0:T(128)S(1)} %sqrt.89, f32[2,4,5,8,256]{4,3,2,1,0:T(8,128)S(1)} %bitcast.190, f32[32]{0:T(128)S(1)} %sqrt.88, f32[32]{0:T(128)S(1)} %get-tuple-element.29, f32[32]{0:T(128)S(1)} %get-tuple-element.28, ...), kind=kOutput, calls=%fused_computation.26 | convolution fusion | flops 671744000 | bytes 16384640 | tf_op jit(solution)/shard_map/ipcnk,dspn->ipcdsk/dot_general | solution.py:102
  194.7 0.6 fusion.43
  195.4 0.5 slice-done.5
  195.9 3.5 %fusion.35 = f32[2,2,32,16,256]{4,2,0,1,3:T(8,128)S(1)} fusion(bf16[16,5,2,256,128]{4,3,2,1,0:T(8,128)(2,1)S(1)} %bitcast.183, f32[16,5,1,32,128]{4,3,1,0,2:T(8,128)S(1)} %get-tuple-element.12, f32[16,5,1,32,128]{4,3,1,0,2:T(8,128)S(1)} %get-tuple-element.11, f32[16,5,128]{2,1,0:T(8,128)S(1)} %copy-done.2), kind=kOutput, calls=%fused_computation.30 | convolution fusion | flops 673054720 | bytes 15245312 | tf_op jit(solution)/shard_map/ipcnk,ipdsk->cdsin/dot_general | solution.py:113
  200.1 1.0 copy.262
  201.1 3.9 %all-to-all-start.7 = ((bf16[32,2,32,128]{3,2,1,0:T(8,128)(2,1)}), bf16[32,2,32,128]{3,2,1,0:T(8,128)(2,1)S(1)}, u32[]{:S(2)}, u32[]{:S(2)}) async-start(bf16[32,2,32,128]{3,2,1,0:T(8,128)(2,1)} %copy.262), calls=%async_computation.7 | async-start | bytes 1048576 | tf_op jit(solution)/shard_map/all_to_all | solution.py:19
  205.1 11.1 %all-to-all-done.7 = bf16[32,2,32,128]{3,2,1,0:T(8,128)(2,1)S(1)} async-done(((bf16[32,2,32,128]{3,2,1,0:T(8,128)(2,1)}), bf16[32,2,32,128]{3,2,1,0:T(8,128)(2,1)S(1)}, u32[]{:S(2)}, u32[]{:S(2)}) %all-to-all-start.7) | async-done | bytes 524320 | tf_op jit(solution)/shard_map/all_to_all | solution.py:19
  216.7 8.9 %all-reduce.8 = f32[128]{0:T(128)S(1)} all-reduce(f32[128]{0:T(128)S(1)} %dynamic-update-slice.8), channel_id=10, replica_groups=mesh['col_0'=4,'col_1'=4,'col_2'=2,'row'=4] {'col_0'}, use_global_device_ids=true, to_apply=%add.8 | all-reduce | flops 128 | bytes 1024
  226.0 9.2 %all-reduce.9 = f32[128]{0:T(128)S(1)} all-reduce(f32[128]{0:T(128)S(1)} %dynamic-update-slice.9), channel_id=11, replica_groups=mesh['col_0'=4,'col_1'=4,'col_2'=2,'row'=4] {'col_1'}, use_global_device_ids=true, to_apply=%add.9 | all-reduce | flops 128 | bytes 1024
  235.5 2.4 all-reduce.10
  238.3 7.7 %all-reduce.11 = f32[128]{0:T(128)S(1)} all-reduce(f32[128]{0:T(128)S(1)} %dynamic-update-slice.11), channel_id=13, replica_groups=mesh['col_0'=4,'col_1'=4,'col_2'=2,'row'=4] {'row'}, use_global_device_ids=true, to_apply=%add.11 | all-reduce | flops 128 | bytes 1024
  246.1 0.6 multiply_multiply_fusion
  246.9 1.0 fusion.87
  247.9 1.8 broadcast_in_dim.68
  249.7 4.2 %all-to-all-start.8 = ((f32[32,2,8,1280]{3,2,1,0:T(8,128)}), f32[32,2,8,1280]{3,2,1,0:T(8,128)S(1)}, u32[]{:S(2)}, u32[]{:S(2)}) async-start(f32[32,2,8,1280]{3,2,1,0:T(8,128)} %broadcast_in_dim.68), calls=%async_computation.8 | async-start | bytes 5242880 | tf_op jit(solution)/shard_map/all_to_all | solution.py:31
  254.2 34.3 %all-to-all-done.8 = f32[32,2,8,1280]{3,2,1,0:T(8,128)S(1)} async-done(((f32[32,2,8,1280]{3,2,1,0:T(8,128)}), f32[32,2,8,1280]{3,2,1,0:T(8,128)S(1)}, u32[]{:S(2)}, u32[]{:S(2)}) %all-to-all-start.8) | async-done | bytes 2621472 | tf_op jit(solution)/shard_map/all_to_all | solution.py:31
  288.5 3.0 copy.263
  291.6 2.7 reshape_reshape.11
  294.3 3.0 copy.264
  297.3 2.3 gather_fusion
  299.7 10.1 %all_to_all.54 = f32[4,2,8,1280]{3,2,1,0:T(8,128)S(1)} all-to-all(f32[4,2,8,1280]{3,2,1,0:T(8,128)S(1)} %broadcast_in_dim.70), channel_id=1, replica_groups=mesh['col_0'=4,'col_1'=4,'col_2'=2,'row'=4] {'row'}, dimensions={0} | all-to-all | bytes 655360 | tf_op jit(solution)/shard_map/all_to_all | solution.py:31
  309.8 0.7 copy.380
  (150 shorter events, 8.5 us)
Async XLA Ops:
  2.3 18.6 %all-to-all-start = ((bf16[32,2,32,128]{3,2,1,0:T(8,128)(2,1)}), bf16[32,2,32,128]{3,2,1,0:T(8,128)(2,1)S(1)}, u32[]{:S(2)}, u32[]{:S(2)}) async-start(bf16[32,2,32,128]{3,2,1,0:T(8,128)(2,1)} %broadcast_in_dim.61), calls=%async_computation | async-start | bytes 1048576 | tf_op jit(solution)/shard_map/all_to_all | solution.py:31
  10.6 83.6 %copy-start.1 = (f32[16,5,128]{2,1,0:T(8,128)}, f32[16,5,128]{2,1,0:T(8,128)S(1)}, u32[]{:S(2)}) copy-start(f32[16,5,128]{2,1,0:T(8,128)S(1)} %fusion.88) | copy-start | bytes 122884
  21.2 6.8 %slice-start.6 = ((s8[10485760]{0:T(1024)(128)(4,1)}), s8[2097152]{0:T(1024)(128)(4,1)S(1)}, s32[]{:S(2)}) async-start(s8[10485760]{0:T(1024)(128)(4,1)} %bitcast.184), calls=%async_computation.16 | async-start | bytes 4194304
  21.4 6.6 %slice-start.7 = ((s8[10485760]{0:T(1024)(128)(4,1)}), s8[4194304]{0:T(1024)(128)(4,1)S(1)}, s32[]{:S(2)}) async-start(s8[10485760]{0:T(1024)(128)(4,1)} %bitcast.184), calls=%async_computation.17 | async-start | bytes 8388608
  21.5 6.9 %slice-start.8 = ((s8[10485760]{0:T(1024)(128)(4,1)}), s8[4194304]{0:T(1024)(128)(4,1)S(1)}, s32[]{:S(2)}) async-start(s8[10485760]{0:T(1024)(128)(4,1)} %bitcast.184), calls=%async_computation.18 | async-start | bytes 8388608
  31.6 6.7 %copy-start.7 = (u32[128]{0:T(128)S(1)}, u32[128]{0:T(128)}, u32[]{:S(2)}) copy-start(u32[128]{0:T(128)} %constant.51) | copy-start | bytes 1540
  31.6 7.9 %copy-start = (f32[2,32,1,128]{3,2,1,0:T(1,128)S(1)}, f32[2,32,1,128]{3,2,1,0:T(1,128)}, u32[]{:S(2)}) copy-start(f32[2,32,1,128]{3,2,1,0:T(1,128)} %param.5) | copy-start | bytes 98308
  31.6 17.2 %copy-start.6 = (u32[128]{0:T(128)S(1)}, u32[128]{0:T(128)}, u32[]{:S(2)}) copy-start(u32[128]{0:T(128)} %constant.56) | copy-start | bytes 1540
  31.6 28.0 %copy-start.5 = (u32[128]{0:T(128)S(1)}, u32[128]{0:T(128)}, u32[]{:S(2)}) copy-start(u32[128]{0:T(128)} %constant.61) | copy-start | bytes 1540
  31.6 32.0 %copy-start.4 = (u32[128]{0:T(128)S(1)}, u32[128]{0:T(128)}, u32[]{:S(2)}) copy-start(u32[128]{0:T(128)} %constant.66) | copy-start | bytes 1540
  32.9 43.4 %all-to-all-start.1 = ((bf16[4,2,32,1280]{3,2,1,0:T(8,128)(2,1)}), bf16[4,2,32,1280]{3,2,1,0:T(8,128)(2,1)S(1)}, u32[]{:S(2)}, u32[]{:S(2)}) async-start(bf16[4,2,32,1280]{3,2,1,0:T(8,128)(2,1)} %broadcast_in_dim.62), calls=%async_computation.1 | async-start | bytes 1310720 | tf_op jit(solution)/shard_map/all_to_all | solution.py:31
  76.3 17.9 %slice-start = ((s8[10485760]{0:T(1024)(128)(4,1)}), s8[2097152]{0:T(1024)(128)(4,1)S(1)}, s32[]{:S(2)}) async-start(s8[10485760]{0:T(1024)(128)(4,1)} %bitcast.180), calls=%async_computation.10 | async-start | bytes 4194304
  87.2 7.1 %slice-start.1 = ((s8[10485760]{0:T(1024)(128)(4,1)}), s8[4194304]{0:T(1024)(128)(4,1)S(1)}, s32[]{:S(2)}) async-start(s8[10485760]{0:T(1024)(128)(4,1)} %bitcast.180), calls=%async_computation.11 | async-start | bytes 8388608
  87.2 7.1 %slice-start.2 = ((s8[10485760]{0:T(1024)(128)(4,1)}), s8[4194304]{0:T(1024)(128)(4,1)S(1)}, s32[]{:S(2)}) async-start(s8[10485760]{0:T(1024)(128)(4,1)} %bitcast.180), calls=%async_computation.12 | async-start | bytes 8388608
  129.7 6.5 %slice-start.9 = ((s8[10485760]{0:T(1024)(128)(4,1)}), s8[2097152]{0:T(1024)(128)(4,1)S(1)}, s32[]{:S(2)}) async-start(s8[10485760]{0:T(1024)(128)(4,1)} %bitcast.186), calls=%async_computation.19 | async-start | bytes 4194304
  130.3 6.0 %slice-start.10 = ((s8[10485760]{0:T(1024)(128)(4,1)}), s8[4194304]{0:T(1024)(128)(4,1)S(1)}, s32[]{:S(2)}) async-start(s8[10485760]{0:T(1024)(128)(4,1)} %bitcast.186), calls=%async_computation.20 | async-start | bytes 8388608
  130.3 6.7 %slice-start.11 = ((s8[10485760]{0:T(1024)(128)(4,1)}), s8[4194304]{0:T(1024)(128)(4,1)S(1)}, s32[]{:S(2)}) async-start(s8[10485760]{0:T(1024)(128)(4,1)} %bitcast.186), calls=%async_computation.21 | async-start | bytes 8388608
  135.6 1.4 copy-start.2
  141.5 36.3 %all-to-all-start.5 = ((bf16[4,2,32,1280]{3,2,1,0:T(8,128)(2,1)}), bf16[4,2,32,1280]{3,2,1,0:T(8,128)(2,1)S(1)}, u32[]{:S(2)}, u32[]{:S(2)}) async-start(bf16[4,2,32,1280]{3,2,1,0:T(8,128)(2,1)} %broadcast_in_dim.66), calls=%async_computation.5 | async-start | bytes 1310720 | tf_op jit(solution)/shard_map/all_to_all | solution.py:31
  177.8 17.6 %slice-start.3 = ((s8[10485760]{0:T(1024)(128)(4,1)}), s8[2097152]{0:T(1024)(128)(4,1)S(1)}, s32[]{:S(2)}) async-start(s8[10485760]{0:T(1024)(128)(4,1)} %bitcast.182), calls=%async_computation.13 | async-start | bytes 4194304
  189.4 6.0 %slice-start.4 = ((s8[10485760]{0:T(1024)(128)(4,1)}), s8[4194304]{0:T(1024)(128)(4,1)S(1)}, s32[]{:S(2)}) async-start(s8[10485760]{0:T(1024)(128)(4,1)} %bitcast.182), calls=%async_computation.14 | async-start | bytes 8388608
  189.4 6.5 %slice-start.5 = ((s8[10485760]{0:T(1024)(128)(4,1)}), s8[4194304]{0:T(1024)(128)(4,1)S(1)}, s32[]{:S(2)}) async-start(s8[10485760]{0:T(1024)(128)(4,1)} %bitcast.182), calls=%async_computation.15 | async-start | bytes 8388608
  201.1 15.1 %all-to-all-start.7 = ((bf16[32,2,32,128]{3,2,1,0:T(8,128)(2,1)}), bf16[32,2,32,128]{3,2,1,0:T(8,128)(2,1)S(1)}, u32[]{:S(2)}, u32[]{:S(2)}) async-start(bf16[32,2,32,128]{3,2,1,0:T(8,128)(2,1)} %copy.262), calls=%async_computation.7 | async-start | bytes 1048576 | tf_op jit(solution)/shard_map/all_to_all | solution.py:19
  249.7 4.2 %copy-start.3 = (s32[160]{0:T(256)S(1)}, s32[160]{0:T(256)}, u32[]{:S(2)}) copy-start(s32[160]{0:T(256)} %param.9) | copy-start | bytes 1924
  249.7 38.8 %all-to-all-start.8 = ((f32[32,2,8,1280]{3,2,1,0:T(8,128)}), f32[32,2,8,1280]{3,2,1,0:T(8,128)S(1)}, u32[]{:S(2)}, u32[]{:S(2)}) async-start(f32[32,2,8,1280]{3,2,1,0:T(8,128)} %broadcast_in_dim.68), calls=%async_computation.8 | async-start | bytes 5242880 | tf_op jit(solution)/shard_map/all_to_all | solution.py:31
